TPU v7x, 256 devices: a whole 4x4x8 slice. The times are simulated.
256 devices in a mesh: fsdp: 16 (over z_hi, y, core), gossip: 16 (over z_lo, x).
Axes of the slice: x: 4, y: 4, z: 8 (z_hi: 2, z_lo: 4; z = z_hi * 4 + z_lo), core: 2. Of those that a mesh axis runs over, the one named last changes fastest.
Arguments:
- tokens: bfloat16 [2, 16, 2048, 5120], P(None, 'gossip', 'fsdp'), may hold values from -0.14941406 to 0.14941406
- master: float32 [16, 5120, 256], P('gossip', 'fsdp'), may hold values from -0.3 to 0.3
- moment: float32 [16, 5120, 256], P('gossip', 'fsdp'), may hold values from -4 to 4
- second: float32 [16, 5120, 256], P('gossip', 'fsdp'), may hold values from 0.1 to 2
- cube_bit: int32 [4], replicated, may hold values from 0 to 2
Outputs:
- averaged: float32 [16, 5120, 256], P('gossip', 'fsdp')
- moment_out: float32 [16, 5120, 256], P('gossip', 'fsdp')
- second_out: float32 [16, 5120, 256], P('gossip', 'fsdp')
Inputs may be any that keep to these rules, and one draw needn't show every extreme that they name: In round r replica g pairs with replica g xor 2^cube_bit[r].
All inputs are finite; a program needn't handle non-finite values.
Results may differ from a plain program's by a relative error of at most 0.006.
Values may be sent and summed in bfloat16 or wider, within the bound.
A program may use at most 64 MiB of HBM per device.

v0:
```python
import jax
import jax.numpy as jnp
from jax import lax
from jax.sharding import PartitionSpec as P


def partner(value, axis, apart):
    mask = 2**apart
    pairs = [(source, source ^ mask) for source in range(lax.axis_size(axis))]
    return lax.ppermute(value, axis, pairs)


def make_swap(which):

    def swapped(value):
        return partner(value, "gossip", which)

    return swapped


def body(tokens, master, moment, second, cube_bit):
    params = master[0]
    first = moment[0]
    squares = second[0]
    width = tokens.shape[3]
    local_rows = tokens.shape[2]
    rank = params.shape[1] // 2
    group_tok = local_rows * lax.axis_size("fsdp")
    position = jnp.arange(local_rows, dtype=jnp.int32)
    keeping = ((position + 1) % local_rows != 0).astype(jnp.float32)[:, None]
    for section in range(tokens.shape[0]):
        gathered = lax.all_gather(params.astype(jnp.bfloat16), "fsdp", axis=0, tiled=True)
        left_part = gathered[:, :rank]
        right_part = gathered[:, rank:]
        xfloat = tokens[section, 0].astype(jnp.float32)
        scaled = xfloat * lax.rsqrt(jnp.mean(xfloat * xfloat, axis=-1, keepdims=True) + 1e-05)
        normed = scaled.astype(jnp.bfloat16)
        low = (
            jnp.dot(normed, left_part, preferred_element_type=jnp.float32) * width ** (-0.5)
        ).astype(jnp.bfloat16)
        out = xfloat + rank ** (-0.5) * jnp.dot(
            low, right_part.T, preferred_element_type=jnp.float32
        )
        inverse = lax.rsqrt(jnp.mean(out * out, axis=-1, keepdims=True) + 1e-05)
        zvalue = out * inverse
        following = jnp.concatenate([scaled[1:], jnp.zeros((1, width), jnp.float32)], axis=0)
        dzvalue = (rank / group_tok) ** 0.5 * (zvalue - following) * keeping
        d_out = (
            inverse * (dzvalue - zvalue * jnp.mean(dzvalue * zvalue, axis=-1, keepdims=True))
        ).astype(jnp.bfloat16)
        d_low = (
            jnp.dot(d_out, right_part, preferred_element_type=jnp.float32)
            * (rank * width) ** (-0.5)
        ).astype(jnp.bfloat16)
        grad = lax.psum_scatter(
            jnp.concatenate(
                [
                    jnp.einsum("td,tr->dr", normed, d_low, preferred_element_type=jnp.float32),
                    jnp.einsum("td,tr->dr", d_out, low, preferred_element_type=jnp.float32)
                    * rank ** (-0.5),
                ],
                axis=1,
            ),
            "fsdp",
            scatter_dimension=0,
            tiled=True,
        )
        first = 0.9 * first + 0.1 * grad
        squares = 0.95 * squares + 0.05 * grad * grad
        params = params - 0.02 * first / (jnp.sqrt(squares) + 1e-08)
    for round_index in range(cube_bit.shape[0]):
        bit_count = lax.axis_size("gossip").bit_length() - 1
        chosen = jnp.clip(cube_bit[round_index], 0, bit_count - 1)
        other = lax.switch(chosen, [make_swap(which) for which in range(bit_count)], params)
        params = 0.5 * (params + other)
    return (params[None], first[None], squares[None])


def solution(mesh):
    in_specs = (
        P(None, "gossip", "fsdp", None),
        P("gossip", "fsdp", None),
        P("gossip", "fsdp", None),
        P("gossip", "fsdp", None),
        P(),
    )
    out_specs = (P("gossip", "fsdp", None), P("gossip", "fsdp", None), P("gossip", "fsdp", None))
    return jax.shard_map(body, mesh=mesh, in_specs=in_specs, out_specs=out_specs, check_vma=False)
```

profile of v0, /device:TPU:2, one launch (start us, length us, event | category | flops | bytes accessed | tf_op | source)
XLA Modules:
  0.0 457.3 jit_solution(939387526671983009)
XLA Ops:
  9.1 2.3 fusion.2
  11.4 2.1 convert_multiply_fusion.2
  15.3 65.7 %all-gather.3.cloned.1.call-done = bf16[5120,256]{1,0:T(8,128)(2,1)} async-done(((bf16[320,256]{1,0:T(8,128)(2,1)}), bf16[5120,256]{1,0:T(8,128)(2,1)}) %all-gather.3.cloned.1.call-update) | async-done | bytes 2621456 | tf_op jit(solution)/shard_map/all_gather | solution.py:32
  89.4 4.3 fusion.39
  93.7 5.4 %pad_maximum_fusion = f32[5120,256]{0,1:T(8,128)} fusion(f32[5120,128]{0,1:T(8,128)} %convolution_multiply_fusion.2, f32[5120,128]{0,1:T(8,128)} %fusion.39), kind=kLoop, calls=%fused_computation.6 | loop fusion | flops 1310720 | bytes 10485760 | tf_op jit(solution)/shard_map/concatenate | solution.py:56
  99.1 6.0 %copy.40 = f32[5120,256]{1,0:T(8,128)} copy(f32[5120,256]{0,1:T(8,128)} %pad_maximum_fusion) | data formatting | bytes 10485760
  105.2 107.9 %reduce-scatter.7.cloned.1.call-done = f32[320,256]{1,0:T(8,128)} async-done(((f32[5120,256]{1,0:T(8,128)}), f32[320,256]{1,0:T(8,128)}) %reduce-scatter.7.cloned.1.call-update) | async-done | bytes 327696 | tf_op jit(solution)/shard_map/reduce_scatter | solution.py:55
  215.1 3.5 slice.53
  218.6 60.5 %all-gather.5.cloned.1.call-done = bf16[5120,256]{1,0:T(8,128)(2,1)} async-done(((bf16[320,256]{1,0:T(8,128)(2,1)}), bf16[5120,256]{1,0:T(8,128)(2,1)}) %all-gather.5.cloned.1.call-update) | async-done | bytes 2621456 | tf_op jit(solution)/shard_map/all_gather | solution.py:32
  285.4 2.1 convolution_multiply_fusion
  287.5 4.3 fusion.42
  291.8 5.5 %pad_maximum_fusion.1 = f32[5120,256]{0,1:T(8,128)} fusion(f32[5120,128]{0,1:T(8,128)} %convolution_multiply_fusion, f32[5120,128]{0,1:T(8,128)} %fusion.42), kind=kLoop, calls=%fused_computation.7 | loop fusion | flops 1310720 | bytes 10485760 | tf_op jit(solution)/shard_map/concatenate | solution.py:56
  297.3 6.0 %copy.42 = f32[5120,256]{1,0:T(8,128)} copy(f32[5120,256]{0,1:T(8,128)} %pad_maximum_fusion.1) | data formatting | bytes 10485760
  307.1 104.1 %reduce-scatter.9.cloned.1.call-done = f32[320,256]{1,0:T(8,128)} async-done(((f32[5120,256]{1,0:T(8,128)}), f32[320,256]{1,0:T(8,128)}) %reduce-scatter.9.cloned.1.call-update) | async-done | bytes 327696 | tf_op jit(solution)/shard_map/reduce_scatter | solution.py:55
  411.3 2.2 fusion.51
  413.5 8.1 %conditional.4 = (f32[320,256]{1,0:T(8,128)}) conditional(s32[]{:T(128)} %bitcast.7, f32[320,256]{1,0:T(8,128)S(1)} %get-tuple-element.47, f32[320,256]{1,0:T(8,128)S(1)} %get-tuple-element.47, f32[320,256]{1,0:T(8,128)S(1)} %get-tuple-element.47, f32[320,256]{1,0:T(8,128)S(1)} %get-tuple-element.47), branch_computations={%region_8.9_spmd, %region_9.10_spmd, %region_10.11_spmd, %region_1... | conditional | bytes 1310768 | solution.py:74
  413.6 8.0 %collective-permute-done.2 = f32[320,256]{1,0:T(8,128)} collective-permute-done((f32[320,256]{1,0:T(8,128)S(1)}, f32[320,256]{1,0:T(8,128)}, u32[]{:S(2)}, u32[]{:S(2)}) %collective-permute-start.2) | collective-permute-done | bytes 327712 | tf_op jit(solution)/shard_map/cond/branch_2_fun/ppermute | solution.py:10
  422.6 8.8 %conditional.5 = (f32[320,256]{1,0:T(8,128)}) conditional(s32[]{:T(128)} %bitcast.8, f32[320,256]{1,0:T(8,128)S(1)} %add_multiply_fusion.2, f32[320,256]{1,0:T(8,128)S(1)} %add_multiply_fusion.2, f32[320,256]{1,0:T(8,128)S(1)} %add_multiply_fusion.2, f32[320,256]{1,0:T(8,128)S(1)} %add_multiply_fusion.2), branch_computations={%region_12.13_spmd, %region_13.14_spmd, %region_14.15_spmd, %regio... | conditional | bytes 1310768 | solution.py:74
  422.6 2.2 collective-permute-start.5
  424.8 6.6 %collective-permute-done.5 = f32[320,256]{1,0:T(8,128)} collective-permute-done((f32[320,256]{1,0:T(8,128)S(1)}, f32[320,256]{1,0:T(8,128)}, u32[]{:S(2)}, u32[]{:S(2)}) %collective-permute-start.5) | collective-permute-done | bytes 327712 | tf_op jit(solution)/shard_map/cond/branch_1_fun/ppermute | solution.py:10
  432.4 8.2 %conditional.6 = (f32[320,256]{1,0:T(8,128)}) conditional(s32[]{:T(128)} %bitcast.9, f32[320,256]{1,0:T(8,128)S(1)} %add_multiply_fusion.1, f32[320,256]{1,0:T(8,128)S(1)} %add_multiply_fusion.1, f32[320,256]{1,0:T(8,128)S(1)} %add_multiply_fusion.1, f32[320,256]{1,0:T(8,128)S(1)} %add_multiply_fusion.1), branch_computations={%region_16.17_spmd, %region_17.18_spmd, %region_18.19_spmd, %regio... | conditional | bytes 1310768 | solution.py:74
  433.1 7.6 %collective-permute-done.8 = f32[320,256]{1,0:T(8,128)} collective-permute-done((f32[320,256]{1,0:T(8,128)S(1)}, f32[320,256]{1,0:T(8,128)}, u32[]{:S(2)}, u32[]{:S(2)}) %collective-permute-start.8) | collective-permute-done | bytes 327712 | tf_op jit(solution)/shard_map/cond/branch_0_fun/ppermute | solution.py:10
  441.7 7.3 %conditional.7 = (f32[320,256]{1,0:T(8,128)}) conditional(s32[]{:T(128)} %bitcast.10, f32[320,256]{1,0:T(8,128)S(1)} %add_multiply_fusion, f32[320,256]{1,0:T(8,128)S(1)} %add_multiply_fusion, f32[320,256]{1,0:T(8,128)S(1)} %add_multiply_fusion, f32[320,256]{1,0:T(8,128)S(1)} %add_multiply_fusion), branch_computations={%region_20.21_spmd, %region_21.22_spmd, %region_22.23_spmd, %regio... | conditional | bytes 1310768 | solution.py:74
  442.3 6.6 %collective-permute-done.12 = f32[320,256]{1,0:T(8,128)} collective-permute-done((f32[320,256]{1,0:T(8,128)S(1)}, f32[320,256]{1,0:T(8,128)}, u32[]{:S(2)}, u32[]{:S(2)}) %collective-permute-start.12) | collective-permute-done | bytes 327712 | tf_op jit(solution)/shard_map/cond/branch_0_fun/ppermute | solution.py:10
  (59 shorter events, 27.8 us)
Async XLA Ops:
  7.2 4.3 copy-start
  7.2 73.8 %all-gather.3.cloned.1.call-start = ((), (), s32[]{:S(2)}) async-start(), calls=%async_computation.2 | async-start | bytes 2785280 | tf_op jit(solution)/shard_map/all_gather | solution.py:32
  9.1 204.0 %reduce-scatter.7.cloned.1.call-start = ((), (), s32[]{:S(2)}) async-start(), calls=%async_computation.4 | async-start | bytes 5570560 | tf_op jit(solution)/shard_map/reduce_scatter | solution.py:55
  81.0 2.1 copy-start.6
  83.2 1.7 copy-start.1
  86.2 1.1 copy-start.4
  105.1 108.0 %copy-start.5 = (f32[1,320,256]{2,1,0:T(8,128)S(1)}, f32[1,320,256]{2,1,0:T(8,128)}, u32[]{:S(2)}) copy-start(f32[1,320,256]{2,1,0:T(8,128)} %param.22) | copy-start | bytes 983044
  105.1 108.0 %copy-start.8 = (f32[1,320,256]{2,1,0:T(8,128)S(1)}, f32[1,320,256]{2,1,0:T(8,128)}, u32[]{:S(2)}) copy-start(f32[1,320,256]{2,1,0:T(8,128)} %param.23) | copy-start | bytes 983044
  105.1 174.0 %all-gather.5.cloned.1.call-start = ((), (), s32[]{:S(2)}) async-start(), calls=%async_computation.3 | async-start | bytes 2785280 | tf_op jit(solution)/shard_map/all_gather | solution.py:32
  215.1 196.2 %reduce-scatter.9.cloned.1.call-start = ((), (), s32[]{:S(2)}) async-start(), calls=%async_computation.5 | async-start | bytes 5570560 | tf_op jit(solution)/shard_map/reduce_scatter | solution.py:55
  279.1 2.1 copy-start.7
  281.3 1.7 copy-start.2
  284.3 1.1 copy-start.3
  303.3 0.7 copy-start.11
  303.3 108.0 %copy-start.9 = (f32[1,320,256]{2,1,0:T(8,128)S(1)}, f32[1,320,256]{2,1,0:T(8,128)}, u32[]{:S(2)}) copy-start(f32[1,320,256]{2,1,0:T(8,128)} %param.24) | copy-start | bytes 983044
  303.3 108.0 %copy-start.10 = (f32[320,256]{1,0:T(8,128)S(1)}, f32[320,256]{1,0:T(8,128)}, u32[]{:S(2)}) copy-start(f32[320,256]{1,0:T(8,128)} %reduce-scatter.7.cloned.1.call-done) | copy-start | bytes 983044
  413.5 8.1 %collective-permute-start.2 = (f32[320,256]{1,0:T(8,128)S(1)}, f32[320,256]{1,0:T(8,128)}, u32[]{:S(2)}, u32[]{:S(2)}) collective-permute-start(f32[320,256]{1,0:T(8,128)S(1)} %param.2), channel_id=1, source_target_pairs={{0,4},{1,5},{2,6},{3,7},{4,0},{5,1},{6,2},{7,3},{8,12},{9,13},{10,... | collective-permute-start | bytes 983048 | tf_op jit(solution)/shard_map/cond/branch_2_fun/ppermute | solution.py:10
  422.6 8.8 %collective-permute-start.5 = (f32[320,256]{1,0:T(8,128)S(1)}, f32[320,256]{1,0:T(8,128)}, u32[]{:S(2)}, u32[]{:S(2)}) collective-permute-start(f32[320,256]{1,0:T(8,128)S(1)} %param.5), channel_id=1, source_target_pairs={{0,2},{1,3},{2,0},{3,1},{4,6},{5,7},{6,4},{7,5},{8,10},{9,11},{10,... | collective-permute-start | bytes 983048 | tf_op jit(solution)/shard_map/cond/branch_1_fun/ppermute | solution.py:10
  432.5 8.2 %collective-permute-start.8 = (f32[320,256]{1,0:T(8,128)S(1)}, f32[320,256]{1,0:T(8,128)}, u32[]{:S(2)}, u32[]{:S(2)}) collective-permute-start(f32[320,256]{1,0:T(8,128)S(1)} %param.8), channel_id=1, source_target_pairs={{0,1},{1,0},{2,3},{3,2},{4,5},{5,4},{6,7},{7,6},{8,9},{9,8},{10,11... | collective-permute-start | bytes 983048 | tf_op jit(solution)/shard_map/cond/branch_0_fun/ppermute | solution.py:10
  441.7 7.3 %collective-permute-start.12 = (f32[320,256]{1,0:T(8,128)S(1)}, f32[320,256]{1,0:T(8,128)}, u32[]{:S(2)}, u32[]{:S(2)}) collective-permute-start(f32[320,256]{1,0:T(8,128)S(1)} %param.12), channel_id=1, source_target_pairs={{0,1},{1,0},{2,3},{3,2},{4,5},{5,4},{6,7},{7,6},{8,9},{9,8},{10,11... | collective-permute-start | bytes 983048 | tf_op jit(solution)/shard_map/cond/branch_0_fun/ppermute | solution.py:10
Sparse Core Ops, SparseCore 0:
  11.3 69.6 all-gather.2
  105.3 107.7 reduce-scatter.6
  216.4 62.6 all-gather.4
  303.4 107.7 reduce-scatter.8
where the time goes:
time: 457 us
  waiting for transfers between devices  367 us (80%)
  other arithmetic  28.7 us (6%)
  local copies, waits for them, and re-layouts  23 us (5%)
  matrix products  18.2 us (4%)
  between operations  16.5 us (4%)
    reduce_scatter x2, waiting for transfers between devices, body(): lax.psum_scatter(jnp.concatenate([jnp.einsum('td,tr->dr', normed, d_low,...  212 us
    all_gather x2, waiting for transfers between devices, body(): lax.all_gather(params.astype(jnp.bfloat16), 'fsdp', axis=0, tiled=True)  126 us
    ppermute x4, waiting for transfers between devices, partner(): return lax.ppermute(value, axis, pairs)  28.9 us
    unnamed x26, local copies, waits for them, and re-layouts  17 us
    concatenate x2, other arithmetic, body(): jnp.concatenate([jnp.einsum('td,tr->dr', normed, d_low, preferred_element...  10.9 us
  transfers between devices with their start and end apart: 8, of which 8 were waited for; matrix products, arithmetic and copies ran while one was open for 2% of the time, Pallas kernels for 0%

commit v1 on v0

v1 whole, which is shorter than its diff:
```python
import jax
import jax.numpy as jnp
from jax import lax
from jax.experimental import pallas as pl
from jax.experimental.pallas import tpu as pltpu
from jax.sharding import PartitionSpec as P

MESH = pl.DeviceIdType.MESH
F32, BF16 = jnp.float32, jnp.bfloat16

D = 5120
RANK = 128
STEPS = 2
DOC = 128
GROUP_TOK = 2048
ROWS = 320
CHIP_ROWS = 640
HALF = 2560
YS = 4
CHUNKS = 2
CHUNK = ROWS // CHUNKS
GROUP = 8
PART = 48


def part_start(member):
    return pl.multiple_of(16 * ((5 * member) // 2), 16)


def kernel(
    tokens, master, moment, second, cube, avg_out, mom_out, sec_out,
    weight, first, squares, wire_w, docs, xs, xt, xgram, pacc, psend, prec, eall,
    keep_cross, keep_own, dsend, drec, zsend, zrec, grec, gsend, arec,
    send_sem, recv_sem, local_sem,
):
    f = lax.axis_index("fsdp")
    g = lax.axis_index("gossip")
    z, y, c = f // 8, (f // 2) % YS, f % 2
    q = g % GROUP

    def at(fi, gi):
        return {"fsdp": fi, "gossip": gi}

    def y_peer(k):
        return (y + k) % YS

    def y_dev(k):
        return at(z * 8 + y_peer(k) * 2 + c, g)

    core_dev = at(z * 8 + y * 2 + (1 - c), g)
    z_dev = at((1 - z) * 8 + y * 2 + c, g)

    def member(delta):
        bits = [(q // (1 << b)) % 2 for b in range(3)]
        return sum((1 - bits[b] if (delta >> b) & 1 else bits[b]) * (1 << b) for b in range(3))

    def gossip_dev(delta):
        return at(f, g - q + member(delta))

    barrier = pltpu.get_barrier_semaphore()
    peers = [y_dev(k) for k in (1, 2, 3)] + [core_dev, z_dev] + [gossip_dev(d) for d in range(1, GROUP)]
    for peer in peers:
        pl.semaphore_signal(barrier, inc=1, device_id=peer, device_id_type=MESH)

    count = [0, 0]
    sent = []

    def remote(src, dst, device):
        i = count[0]
        count[0] += 1
        copy = pltpu.make_async_remote_copy(
            src_ref=src, dst_ref=dst, send_sem=send_sem.at[i], recv_sem=recv_sem.at[i],
            device_id=device, device_id_type=MESH,
        )
        copy.start()
        sent.append(copy)
        return copy

    def local(src, dst):
        i = count[1]
        count[1] += 1
        copy = pltpu.make_async_copy(src, dst, local_sem.at[i])
        copy.start()
        return copy

    def token_block(s, p, who):
        return tokens.at[s, 0, :, pl.ds(pl.multiple_of(p * HALF + who * CHIP_ROWS, 128), CHIP_ROWS)]

    def doc_rows(who):
        return pl.ds(pl.multiple_of(who * DOC, DOC), DOC)

    in_weight = local(master.at[0], weight)
    in_doc = [local(tokens.at[s, 0], docs.at[s]) for s in range(STEPS)]
    in_own = [[local(token_block(s, p, y), xs.at[s, p, doc_rows(y), :]) for p in (0, 1)] for s in range(STEPS)]
    in_first = local(moment.at[0], first)
    in_squares = local(second.at[0], squares)

    def send_tokens(s):
        return {
            k: [remote(token_block(s, p, y_peer(k)), xs.at[s, p, doc_rows(y), :], y_dev(k)) for p in (0, 1)]
            for k in (1, 3, 2)
        }

    def rows_of(core, chunk=0, size=ROWS):
        return pl.ds(pl.multiple_of(core * ROWS + chunk * CHUNK, 32), size)

    def send_weights(s, chunk):
        own = wire_w.at[s, z, rows_of(c, chunk, CHUNK), :]
        return remote(own, own, z_dev), remote(own, own, core_dev)

    def forward_weights(s, chunk):
        got = wire_w.at[s, 1 - z, rows_of(c, chunk, CHUNK), :]
        return remote(got, got, core_dev)

    in_weight.wait()
    wire_w[0, z, rows_of(c), :] = weight[...].astype(BF16)
    pl.semaphore_wait(barrier, len(peers))

    tok_copies = [None] * STEPS
    w_copies = [send_weights(0, chunk) for chunk in range(CHUNKS)]
    tok_copies[0] = send_tokens(0)

    m = D**-0.5
    r = RANK**-0.5
    alpha = (RANK / GROUP_TOK) ** 0.5
    tall = (DOC, RANK)

    def gram_of(s):
        in_doc[s].wait()
        x = docs[s]
        xgram[s] = lax.dot_general(x, x, (((1,), (1,)), ((), ())), preferred_element_type=F32)

    gram_of(0)

    for s in range(STEPS):
        for chunk in range(CHUNKS):
            w_copies[chunk][1].wait_recv()
        forwards = []
        for chunk in range(CHUNKS):
            w_copies[chunk][0].wait_recv()
            forwards.append(forward_weights(s, chunk))
        for copy in in_own[s]:
            copy.wait()
        for copy in forwards:
            copy.wait_recv()
        gram = jnp.zeros((RANK, RANK), F32)
        for p in (0, 1):
            right = wire_w[s, p, :, RANK:]
            gram += lax.dot_general(right, right, (((0,), (0,)), ((), ())), preferred_element_type=F32)
        gram_wire = gram.astype(BF16)

        def product(who):
            return sum(
                jnp.dot(xs[s, p, doc_rows(who), :], wire_w[s, p], preferred_element_type=F32) for p in (0, 1)
            )

        p_copies = []
        for k in (1, 3, 2):
            for copy in tok_copies[s][YS - k]:
                copy.wait_recv()
            psend[s, k - 1, :, : 2 * RANK] = product(y_peer(k)).astype(BF16)
            psend[s, k - 1, :, 2 * RANK :] = gram_wire
            p_copies.append(remote(psend.at[s, k - 1], prec.at[s, k - 1], y_dev(k)))
        prod = product(y)

        for p in (0, 1):
            xt[p] = xs[s, p].T

        at_t = lax.broadcasted_iota(jnp.int32, tall, 0)
        at_j = lax.broadcasted_iota(jnp.int32, tall, 1)
        xx = xgram[s]
        sx = jnp.sum(jnp.where(at_j == at_t, xx, 0.0), axis=1, keepdims=True)
        xn = jnp.sum(jnp.where(at_j == at_t + 1, xx, 0.0), axis=1, keepdims=True)
        ix = lax.rsqrt(sx * (1.0 / D) + 1e-5)
        ixn = pltpu.roll(jnp.broadcast_to(ix, tall), DOC - 1, 0)[:, :1]
        kept = jnp.where(lax.broadcasted_iota(jnp.int32, (DOC, 1), 0) == DOC - 1, 0.0, alpha)

        for copy in p_copies:
            copy.wait_recv()
        for k in range(3):
            prod += prec[s, k, :, : 2 * RANK].astype(F32)
            gram += prec[s, k, :, 2 * RANK :].astype(F32)

        pl_, pr = prod[:, :RANK], prod[:, RANK:]
        prn = pltpu.roll(pr, DOC - 1, 0)
        low = (ix * pl_ * m).astype(BF16)
        lowf = low.astype(F32)
        ghi = gram.astype(BF16)
        glo = (gram - ghi.astype(F32)).astype(BF16)
        lowg = jnp.dot(low, ghi, preferred_element_type=F32) + jnp.dot(low, glo, preferred_element_type=F32)
        oo = (
            sx
            + (2 * r) * jnp.sum(lowf * pr, axis=1, keepdims=True)
            + (r * r) * jnp.sum(lowf * lowg, axis=1, keepdims=True)
        )
        inv = lax.rsqrt(oo * (1.0 / D) + 1e-5)
        sno = ixn * (xn + r * jnp.sum(lowf * prn, axis=1, keepdims=True))
        cc = kept * (inv * inv * oo - inv * sno) * (1.0 / D)
        aa = inv * inv * (kept - cc)
        bb = kept * inv * ixn
        al = aa * lowf
        dlow = (aa * (pr + r * lowg) - bb * prn) * (RANK * D) ** -0.5
        eall[s, y, :, :RANK] = (ix * dlow).astype(BF16)
        eall[s, y, :, RANK : 2 * RANK] = (r * (al - pltpu.roll(bb * lowf, 1, 0))).astype(BF16)
        eall[s, y, :, 2 * RANK :] = (
            (r * r)
            * lax.dot_general(low, al.astype(BF16), (((0,), (0,)), ((), ())), preferred_element_type=F32)
        ).astype(BF16)
        e_copies = [remote(eall.at[s, y], eall.at[s, y], y_dev(k)) for k in (1, 3, 2)]
        for copy in e_copies:
            copy.wait_recv()
        if s + 1 < STEPS:
            tok_copies[s + 1] = send_tokens(s + 1)

        factor = jnp.concatenate([eall[s, j, :, : 2 * RANK] for j in range(YS)], axis=0)
        outer = sum(eall[s, j, :, 2 * RANK :].astype(F32) for j in range(YS)).astype(BF16)

        def gradient(p, core):
            rows = jnp.dot(xt[p, rows_of(core), :], factor, preferred_element_type=F32)
            more = jnp.dot(wire_w[s, p, rows_of(core), RANK:], outer, preferred_element_type=F32)
            return jnp.concatenate([rows[:, :RANK], rows[:, RANK:] + more], axis=1)

        dsend[s, 0] = gradient(1 - z, 1 - c).astype(BF16)
        cross = remote(dsend.at[s, 0], drec.at[s, 0], core_dev)
        keep_cross[...] = gradient(1 - z, c)
        cross.wait_recv()
        z_copies = []
        for chunk in range(CHUNKS):
            part = pl.ds(chunk * CHUNK, CHUNK)
            zsend[s, part, :] = (keep_cross[part, :] + drec[s, 0, part, :].astype(F32)).astype(BF16)
            z_copies.append(remote(zsend.at[s, part, :], zrec.at[s, part, :], z_dev))
        dsend[s, 1] = gradient(z, 1 - c).astype(BF16)
        own = remote(dsend.at[s, 1], drec.at[s, 1], core_dev)
        keep_own[...] = gradient(z, c)
        own.wait_recv()
        keep_own[...] += drec[s, 1].astype(F32)

        if s == 0:
            in_first.wait()
            in_squares.wait()
            gram_of(1)
        w_copies = []
        for chunk in range(CHUNKS):
            part = pl.ds(chunk * CHUNK, CHUNK)
            z_copies[chunk].wait_recv()
            grad = keep_own[part, :] + zrec[s, part, :].astype(F32)
            one = 0.9 * first[part, :] + 0.1 * grad
            two = 0.95 * squares[part, :] + 0.05 * grad * grad
            new = weight[part, :] - 0.02 * one / (jnp.sqrt(two) + 1e-8)
            first[part, :] = one
            squares[part, :] = two
            weight[part, :] = new
            wire_w[s + 1, z, rows_of(c, chunk, CHUNK), :] = new.astype(BF16)
            if s + 1 < STEPS:
                w_copies.append(send_weights(s + 1, chunk))

    out_first = local(first, mom_out.at[0])
    out_squares = local(squares, sec_out.at[0])

    g_copies = []
    for delta in range(1, GROUP):
        start = c * ROWS + part_start(member(delta))
        rows = pl.ds(pl.multiple_of(start, 16), PART)
        g_copies.append(remote(wire_w.at[STEPS, z, rows, :], grec.at[delta - 1], gossip_dev(delta)))
    share = []
    for b in range(3):
        used = sum((cube[i] == b).astype(jnp.int32) for i in range(4))
        share.append(0.5 * jnp.minimum(used, 1).astype(F32))
    held = [weight[pl.ds(part_start(q), PART), :]]
    for delta in range(1, GROUP):
        g_copies[delta - 1].wait_recv()
        held.append(grec[delta - 1].astype(F32))
    for b in range(3):
        held = [held[d] + share[b] * (held[d ^ (1 << b)] - held[d]) for d in range(GROUP)]
    a_copies = []
    for delta in range(1, GROUP):
        gsend[delta - 1] = held[delta].astype(BF16)
        a_copies.append(remote(gsend.at[delta - 1], arec.at[delta - 1], gossip_dev(delta)))
    avg_out[0, pl.ds(part_start(q), PART), :] = held[0]
    for delta in range(1, GROUP):
        a_copies[delta - 1].wait_recv()
        avg_out[0, pl.ds(part_start(member(delta)), PART), :] = arec[delta - 1].astype(F32)

    for copy in sent:
        copy.wait_send()
    out_first.wait()
    out_squares.wait()


def body(tokens, master, moment, second, cube_bit):
    any_space = pl.BlockSpec(memory_space=pl.ANY)
    vmem = pl.BlockSpec(memory_space=pltpu.VMEM)
    rows = jax.ShapeDtypeStruct((1, ROWS, 2 * RANK), F32)
    wide = 3 * RANK
    n_remote = 3 * STEPS * CHUNKS + STEPS * (6 + 3 + 3 + 2 + CHUNKS) + 2 * (GROUP - 1)
    scratch = [
        pltpu.VMEM((ROWS, 2 * RANK), F32),
        pltpu.VMEM((ROWS, 2 * RANK), F32),
        pltpu.VMEM((ROWS, 2 * RANK), F32),
        pltpu.VMEM((STEPS + 1, 2, CHIP_ROWS, 2 * RANK), BF16),
        pltpu.VMEM((STEPS, DOC, D), BF16),
        pltpu.VMEM((STEPS, 2, YS * DOC, CHIP_ROWS), BF16),
        pltpu.VMEM((2, CHIP_ROWS, YS * DOC), BF16),
        pltpu.VMEM((STEPS, DOC, DOC), F32),
        pltpu.VMEM((DOC, 2 * RANK), F32),
        pltpu.VMEM((STEPS, 3, DOC, wide), BF16),
        pltpu.VMEM((STEPS, 3, DOC, wide), BF16),
        pltpu.VMEM((STEPS, YS, DOC, wide), BF16),
        pltpu.VMEM((ROWS, 2 * RANK), F32),
        pltpu.VMEM((ROWS, 2 * RANK), F32),
        pltpu.VMEM((STEPS, 2, ROWS, 2 * RANK), BF16),
        pltpu.VMEM((STEPS, 2, ROWS, 2 * RANK), BF16),
        pltpu.VMEM((STEPS, ROWS, 2 * RANK), BF16),
        pltpu.VMEM((STEPS, ROWS, 2 * RANK), BF16),
        pltpu.VMEM((GROUP - 1, PART, 2 * RANK), BF16),
        pltpu.VMEM((GROUP - 1, PART, 2 * RANK), BF16),
        pltpu.VMEM((GROUP - 1, PART, 2 * RANK), BF16),
        pltpu.SemaphoreType.DMA((n_remote,)),
        pltpu.SemaphoreType.DMA((n_remote,)),
        pltpu.SemaphoreType.DMA((3 + 3 * STEPS + 2,)),
    ]
    return pl.pallas_call(
        kernel,
        out_shape=(rows, rows, rows),
        in_specs=[any_space] * 4 + [pl.BlockSpec(memory_space=pltpu.SMEM)],
        out_specs=(vmem, any_space, any_space),
        scratch_shapes=scratch,
        compiler_params=pltpu.CompilerParams(
            collective_id=0, has_side_effects=True, vmem_limit_bytes=40 * 1024 * 1024
        ),
        name="train",
    )(tokens, master, moment, second, cube_bit)


def solution(mesh):
    in_specs = (
        P(None, "gossip", "fsdp", None),
        P("gossip", "fsdp", None),
        P("gossip", "fsdp", None),
        P("gossip", "fsdp", None),
        P(),
    )
    out_specs = (P("gossip", "fsdp", None), P("gossip", "fsdp", None), P("gossip", "fsdp", None))
    return jax.shard_map(body, mesh=mesh, in_specs=in_specs, out_specs=out_specs, check_vma=False)
```

time: 457 us -> 106 us (0.23)
  waiting for transfers between devices: 367 us -> 0 us
  Pallas kernels: 0 us -> 97.4 us
  other arithmetic: 28.7 us -> 0 us
  matrix products: 18.2 us -> 0 us
  between operations: 16.5 us -> 0.65 us
  local copies, waits for them, and re-layouts: 23 us -> 7.48 us
    reduce_scatter x2 -> x0, waiting for transfers between devices: 212 us -> none  [body(): lax.psum_scatter(jnp.concatenate([jnp.einsum('td,tr->dr', normed, d_low,...]
    all_gather x2 -> x0, waiting for transfers between devices: 126 us -> none  [body(): lax.all_gather(params.astype(jnp.bfloat16), 'fsdp', axis=0, tiled=True)]
    pallas_call x0 -> x1, Pallas kernels: none -> 97.4 us  [body(): pl.pallas_call(kernel, out_shape=(rows, rows, rows), in_specs=[any_space]...]
    ppermute x4 -> x0, waiting for transfers between devices: 28.9 us -> none  [partner(): return lax.ppermute(value, axis, pairs)]
    dot_general x8 -> x0, matrix products: 18.2 us -> none  [the longest x2 8.6 us: body(): jnp.einsum('td,tr->dr', normed, d_low, preferred_element_type=jnp.float32)]
    concatenate x2 -> x0, other arithmetic: 10.9 us -> none  [body(): jnp.concatenate([jnp.einsum('td,tr->dr', normed, d_low, preferred_element...]
    unnamed x26 -> x13, local copies, waits for them, and re-layouts: 17 us -> 7.48 us
    slice x3 -> x0, local copies, waits for them, and re-layouts: 5.92 us -> none  [the longest x2 5.3 us: body(): scaled[1:]]
  transfers between devices with their start and end apart: 8 -> 0, of which waited for: 8 -> 0; matrix products, arithmetic and copies ran while one was open for 2% -> 0% of each run, Pallas kernels for 0% -> 0%
where the time goes in v1:
time: 106 us
  Pallas kernels  97.4 us (92%)
  local copies, waits for them, and re-layouts  7.48 us (7%)
    pallas_call x1, Pallas kernels, body(): pl.pallas_call(kernel, out_shape=(rows, rows, rows), in_specs=[any_space]...  97.4 us
    unnamed x13, local copies, waits for them, and re-layouts  7.48 us

profile of v1, /device:TPU:2, one launch (start us, length us, event | category | flops | bytes accessed | tf_op | source)
XLA Modules:
  0.0 105.5 jit_solution(2175039465362546272)
XLA Ops:
  0.6 0.0 copy-start
  0.6 1.7 %copy-done = bf16[2,1,128,5120]{3,2,1,0:T(8,128)(2,1)S(1)} copy-done((bf16[2,1,128,5120]{3,2,1,0:T(8,128)(2,1)S(1)}, bf16[2,1,128,5120]{3,2,1,0:T(8,128)(2,1)}, u32[]{:S(2)}) %copy-start) | copy-done | bytes 2621464
  2.4 0.0 copy-start.1
  2.4 1.0 copy-done.1
  3.3 0.0 copy-start.2
  3.3 1.0 copy-done.2
  4.3 0.0 copy-start.3
  4.3 1.0 copy-done.3
  5.3 0.0 copy-start.4
  5.3 0.7 copy-done.4
  5.9 97.4 %train.1 = (f32[1,320,256]{2,1,0:T(8,128)S(1)}, f32[1,320,256]{2,1,0:T(8,128)S(1)}, f32[1,320,256]{2,1,0:T(8,128)S(1)}) custom-call(bf16[2,1,128,5120]{3,2,1,0:T(8,128)(2,1)S(1)} %copy-done, f32[1,320,256]{2,1,0:T(8,128)S(1)} %copy-done.1, f32[1,320,256]{2,1,0:T(8,128)S(1)} %copy-done.2, f32[1,320,256]{2,1,0:T(8,128)S(1)} %copy-done.3, s32[4]{0:T(128)S(1)} %copy-done.4), custom_call_target="tpu_custom_call" | custom-call | tf_op jit(solution)/shard_map/train/pallas_call | solution.py:322
  103.3 0.7 copy.11
  104.1 0.7 copy.12
  104.8 0.7 copy.13
Async XLA Ops:
  0.6 1.7 %copy-start = (bf16[2,1,128,5120]{3,2,1,0:T(8,128)(2,1)S(1)}, bf16[2,1,128,5120]{3,2,1,0:T(8,128)(2,1)}, u32[]{:S(2)}) copy-start(bf16[2,1,128,5120]{3,2,1,0:T(8,128)(2,1)} %tokens.1) | copy-start | bytes 7864324
  2.4 1.0 copy-start.1
  3.3 1.0 copy-start.2
  4.3 1.0 copy-start.3
  5.3 0.7 copy-start.4

commit v2 on v0

v2 whole, which is shorter than its diff:
```python
import math

import jax
import jax.numpy as jnp
from jax import lax
from jax.experimental import pallas as pl
from jax.experimental.pallas import tpu as pltpu
from jax.sharding import PartitionSpec as P

MESH = pl.DeviceIdType.MESH
F32, BF16 = jnp.float32, jnp.bfloat16

D = 5120
RANK = 128
STEPS = 2
DOC = 128
GROUP_TOK = 2048
ROWS = 320
CHIP_ROWS = 640
HALF = 2560
YS = 4
GROUP = 8
PART = 48
N_GROUPS = 46
N_LOCAL = 13
BULK = 12288
VMEM_LIMIT = 60 * 1024 * 1024
OTHERS = (1, 3, 2)


def part_start(member):
    return pl.multiple_of(16 * ((5 * member) // 2), 16)


def kernel(
    tokens, master, moment, second, cube, avg_out, mom_out, sec_out,
    weight, first, squares, wire, docs, xs, xt, xgram, pacc, gram_send, gram_recv, psend, prec, eall, right,
    keep_cross, keep_own, dsend, drec, zsend, zrec, grec, gsend, arec, averaged,
    bulk, send_sem, recv_sem, local_sem, near_sem, far_sem,
):
    f = lax.axis_index("fsdp")
    g = lax.axis_index("gossip")
    z, y, c = f // 8, (f // 2) % YS, f % 2
    q = g % GROUP

    def at(fi, gi):
        return {"fsdp": fi, "gossip": gi}

    def y_peer(k):
        return (y + k) % YS

    def y_dev(k):
        return at(z * 8 + y_peer(k) * 2 + c, g)

    core_dev = at(z * 8 + y * 2 + (1 - c), g)
    z_dev = at((1 - z) * 8 + y * 2 + c, g)

    def member(delta):
        bits = [(q // (1 << b)) % 2 for b in range(3)]
        return sum((1 - bits[b] if (delta >> b) & 1 else bits[b]) * (1 << b) for b in range(3))

    def gossip_dev(delta):
        return at(f, g - q + member(delta))

    barrier = pltpu.get_barrier_semaphore()

    def signal(sem, device):
        pl.semaphore_signal(sem, inc=1, device_id=device, device_id_type=MESH)

    for k in OTHERS:
        signal(barrier, at(z * 8 + y_peer(k) * 2, g))

    @pl.when(c == 1)
    def _():
        signal(barrier, core_dev)

    signal(barrier, at((1 - z) * 8 + y * 2 + 1, g))
    for delta in range(1, GROUP):
        signal(barrier, at(z * 8 + y * 2 + 1, g - q + member(delta)))

    def near_ready():
        @pl.when(c == 0)
        def _():
            pl.semaphore_wait(barrier, 2 * YS - 1)
            signal(near_sem, core_dev)

        @pl.when(c == 1)
        def _():
            pl.semaphore_wait(near_sem, 1)

    def far_ready():
        @pl.when(c == 1)
        def _():
            pl.semaphore_wait(barrier, 2 * GROUP)
            signal(far_sem, core_dev)

        @pl.when(c == 0)
        def _():
            pl.semaphore_wait(far_sem, 1)

    count = [0, 0]
    stage = [0]
    bytes_sent = [0] * (STEPS + 1)

    def new_group():
        count[0] += 1
        return count[0] - 1

    def remote(src, dst, device, group):
        pltpu.make_async_remote_copy(
            src_ref=src, dst_ref=dst, send_sem=send_sem.at[stage[0]], recv_sem=recv_sem.at[group],
            device_id=device, device_id_type=MESH,
        ).start()
        rows = math.prod(src.shape) // RANK
        bytes_sent[stage[0]] += rows

    def arrive(group, like):
        pltpu.make_async_remote_copy(
            src_ref=like, dst_ref=like, send_sem=send_sem.at[0], recv_sem=recv_sem.at[group],
            device_id=core_dev, device_id_type=MESH,
        ).wait_recv()

    def flush(which):
        like = bulk.at[pl.ds(0, bytes_sent[which]), :]
        pltpu.make_async_remote_copy(
            src_ref=like, dst_ref=like, send_sem=send_sem.at[which], recv_sem=recv_sem.at[0],
            device_id=core_dev, device_id_type=MESH,
        ).wait_send()
        bytes_sent[which] = 0

    def loaded(copy):
        copy.wait()

    def local(src, dst):
        i = count[1]
        count[1] += 1
        copy = pltpu.make_async_copy(src, dst, local_sem.at[i])
        copy.start()
        return copy

    def feature_cols(p, who):
        return pl.ds(pl.multiple_of(p * HALF + who * CHIP_ROWS, 128), CHIP_ROWS)

    def doc_rows(who):
        return pl.ds(pl.multiple_of(who * DOC, DOC), DOC)

    def rows_of(core):
        return pl.ds(pl.multiple_of(core * ROWS, 64), ROWS)

    def cols(h):
        return slice(h * RANK, (h + 1) * RANK)

    def dot(a, b):
        return jnp.dot(a, b, preferred_element_type=F32)

    def tdot(a, b):
        return lax.dot_general(a, b, (((0,), (0,)), ((), ())), preferred_element_type=F32)

    def send_tokens(s):
        groups = {}
        for k in OTHERS:
            groups[k] = new_group()
            for p in (0, 1):
                remote(
                    docs.at[s, :, feature_cols(p, y_peer(k))], xs.at[s, p, doc_rows(y), :], y_dev(k), groups[k]
                )
        return groups

    def send_weights(s, h):
        own = wire.at[s, h, z, rows_of(c), :]
        groups = new_group(), new_group()
        remote(own, own, z_dev, groups[0])
        remote(own, own, core_dev, groups[1])
        return groups

    def forward_weights(s, h):
        got = wire.at[s, h, 1 - z, rows_of(c), :]
        group = new_group()
        arrive(w_groups[h][0], got)
        remote(got, got, core_dev, group)
        return group

    def weights_here(group, s, h, p):
        arrive(group, wire.at[s, h, p, rows_of(1 - c), :])

    in_weight = local(master.at[0], weight)
    in_doc = [local(tokens.at[0, 0], docs.at[0])]
    loaded(in_weight)
    for h in (0, 1):
        wire[0, h, z, rows_of(c), :] = weight[:, cols(h)].astype(BF16)
    loaded(in_doc[0])
    near_ready()
    tok_groups = [send_tokens(0)]
    far_ready()
    w_groups = [send_weights(0, h) for h in (0, 1)]
    in_doc.append(local(tokens.at[1, 0], docs.at[1]))
    in_own = [
        [local(tokens.at[s, 0, :, feature_cols(p, y)], xs.at[s, p, doc_rows(y), :]) for p in (0, 1)]
        for s in range(STEPS)
    ]
    in_first = local(moment.at[0], first)
    in_squares = local(second.at[0], squares)

    m = D**-0.5
    r = RANK**-0.5
    alpha = (RANK / GROUP_TOK) ** 0.5
    tall = (DOC, RANK)

    def gram_of(s):
        x = docs[s]
        xgram[s] = lax.dot_general(x, x, (((1,), (1,)), ((), ())), preferred_element_type=F32)

    gram_of(0)

    for s in range(STEPS):

        def part_product(who, h, p):
            return dot(xs[s, p, doc_rows(who), :], wire[s, h, p])

        def part_gram(p):
            right[...] = wire[s, 1, p]
            return tdot(right[...], right[...])

        def tokens_here(k):
            arrive(tok_groups[s][k], xs.at[s, :, doc_rows((y + YS - k) % YS), :])

        gram_group, p_groups = new_group(), (new_group(), new_group())

        def send_gram(gram):
            gram_send[s] = gram.astype(BF16)
            for k in OTHERS:
                remote(gram_send.at[s], gram_recv.at[s, k - 1], y_dev(k), gram_group)

        def send_product(k, h, value):
            psend[s, h, k - 1] = value.astype(BF16)
            remote(psend.at[s, h, k - 1], prec.at[s, h, k - 1], y_dev(k), p_groups[h])

        if s == 0:
            forwards = [forward_weights(s, h) for h in (0, 1)]
            for h in (0, 1):
                weights_here(w_groups[h][1], s, h, z)
                weights_here(forwards[h], s, h, 1 - z)
            gram = part_gram(0) + part_gram(1)
            send_gram(gram)
            for copy in in_own[s]:
                loaded(copy)
            for k in OTHERS:
                tokens_here(YS - k)
                for h in (0, 1):
                    send_product(k, h, part_product(y_peer(k), h, 0) + part_product(y_peer(k), h, 1))
            for h in (0, 1):
                pacc[h, 0] = part_product(y, h, 0) + part_product(y, h, 1)
        else:
            for copy in in_own[s]:
                loaded(copy)
            for k in OTHERS:
                tokens_here(k)
            weights_here(w_groups[0][1], s, 0, z)
            for k in range(YS):
                pacc[0, k] = part_product(y_peer(k), 0, z)
            weights_here(forward_weights(s, 0), s, 0, 1 - z)
            for k in OTHERS:
                send_product(k, 0, pacc[0, k] + part_product(y_peer(k), 0, 1 - z))
            pacc[0, 0] += part_product(y, 0, 1 - z)
            weights_here(w_groups[1][1], s, 1, z)
            for k in range(YS):
                pacc[1, k] = part_product(y_peer(k), 1, z)
            gram = part_gram(z)
            weights_here(forward_weights(s, 1), s, 1, 1 - z)
            gram += part_gram(1 - z)
            send_gram(gram)
            for k in OTHERS:
                send_product(k, 1, pacc[1, k] + part_product(y_peer(k), 1, 1 - z))
            pacc[1, 0] += part_product(y, 1, 1 - z)

        for p in (0, 1):
            xt[p] = xs[s, p].T
        at_t = lax.broadcasted_iota(jnp.int32, tall, 0)
        at_j = lax.broadcasted_iota(jnp.int32, tall, 1)
        xx = xgram[s]
        sx = jnp.sum(jnp.where(at_j == at_t, xx, 0.0), axis=1, keepdims=True)
        xn = jnp.sum(jnp.where(at_j == at_t + 1, xx, 0.0), axis=1, keepdims=True)
        ix = lax.rsqrt(sx * (1.0 / D) + 1e-5)
        ixn = pltpu.roll(jnp.broadcast_to(ix, tall), DOC - 1, 0)[:, :1]
        kept = jnp.where(lax.broadcasted_iota(jnp.int32, (DOC, 1), 0) == DOC - 1, 0.0, alpha)

        arrive(gram_group, gram_recv.at[s])
        for k in range(3):
            gram += gram_recv[s, k].astype(F32)
        ghi = gram.astype(BF16)
        glo = (gram - ghi.astype(F32)).astype(BF16)
        arrive(p_groups[0], prec.at[s, 0])
        left = pacc[0, 0]
        for k in range(3):
            left += prec[s, 0, k].astype(F32)
        low = (ix * left * m).astype(BF16)
        lowf = low.astype(F32)
        lowg = dot(low, ghi) + dot(low, glo)
        arrive(p_groups[1], prec.at[s, 1])
        pr = pacc[1, 0]
        for k in range(3):
            pr += prec[s, 1, k].astype(F32)

        prn = pltpu.roll(pr, DOC - 1, 0)
        oo = (
            sx
            + (2 * r) * jnp.sum(lowf * pr, axis=1, keepdims=True)
            + (r * r) * jnp.sum(lowf * lowg, axis=1, keepdims=True)
        )
        inv = lax.rsqrt(oo * (1.0 / D) + 1e-5)
        sno = ixn * (xn + r * jnp.sum(lowf * prn, axis=1, keepdims=True))
        cc = kept * (inv * inv * oo - inv * sno) * (1.0 / D)
        aa = inv * inv * (kept - cc)
        bb = kept * inv * ixn
        dlow = (aa * (pr + r * lowg) - bb * prn) * (RANK * D) ** -0.5
        e_groups = []

        def send_factor(kind, value):
            eall[s, kind, y] = value.astype(BF16)
            e_groups.append(new_group())
            for k in OTHERS:
                remote(eall.at[s, kind, y], eall.at[s, kind, y], y_dev(k), e_groups[kind])

        send_factor(0, ix * dlow)
        al = aa * lowf
        send_factor(1, r * (al - pltpu.roll(bb * lowf, 1, 0)))
        send_factor(2, (r * r) * tdot(low, al.astype(BF16)))
        if s + 1 < STEPS:
            stage[0] = s + 1
            loaded(in_doc[s + 1])
            tok_groups.append(send_tokens(s + 1))

        own_groups = []
        z_groups = []
        for h in (0, 1):
            for kind in (0,) if h == 0 else (1, 2):
                arrive(e_groups[kind], eall.at[s, kind, pl.ds(0, YS - 1)])
            factor = eall[s, h].reshape(YS * DOC, RANK)
            if h == 1:
                outer = sum(eall[s, 2, j].astype(F32) for j in range(YS)).astype(BF16)

            def gradient(p, core):
                rows = dot(xt[p, rows_of(core), :], factor)
                if h == 1:
                    rows += dot(wire[s, 1, p, rows_of(core), :], outer)
                return rows

            dsend[s, h, 0] = gradient(1 - z, 1 - c).astype(BF16)
            cross = new_group()
            remote(dsend.at[s, h, 0], drec.at[s, h, 0], core_dev, cross)
            keep_cross[...] = gradient(1 - z, c)
            dsend[s, h, 1] = gradient(z, 1 - c).astype(BF16)
            own_groups.append(new_group())
            remote(dsend.at[s, h, 1], drec.at[s, h, 1], core_dev, own_groups[h])
            arrive(cross, drec.at[s, h, 0])
            zsend[s, h] = (keep_cross[...] + drec[s, h, 0].astype(F32)).astype(BF16)
            z_groups.append(new_group())
            remote(zsend.at[s, h], zrec.at[s, h], z_dev, z_groups[h])
            keep_own[h] = gradient(z, c)
        if s == 0:
            loaded(in_first)
            loaded(in_squares)
            gram_of(1)
        for h in (0, 1):
            arrive(own_groups[h], drec.at[s, h, 1])
            keep_own[h] += drec[s, h, 1].astype(F32)
        w_groups = []
        g_groups = []
        if s + 1 == STEPS:
            stage[0] = STEPS
        for h in (0, 1):
            arrive(z_groups[h], zrec.at[s, h])
            grad = keep_own[h] + zrec[s, h].astype(F32)
            one = 0.9 * first[:, cols(h)] + 0.1 * grad
            two = 0.95 * squares[:, cols(h)] + 0.05 * grad * grad
            new = weight[:, cols(h)] - 0.02 * one / (jnp.sqrt(two) + 1e-8)
            first[:, cols(h)] = one
            squares[:, cols(h)] = two
            weight[:, cols(h)] = new
            wire[s + 1, h, z, rows_of(c), :] = new.astype(BF16)
            if s + 1 < STEPS:
                w_groups.append(send_weights(s + 1, h))
                continue
            g_groups.append(new_group())
            for delta in range(1, GROUP):
                start = c * ROWS + part_start(member(delta))
                rows = pl.ds(pl.multiple_of(start, 16), PART)
                remote(wire.at[STEPS, h, z, rows, :], grec.at[h, delta - 1], gossip_dev(delta), g_groups[h])

    outs = [local(first, mom_out.at[0]), local(squares, sec_out.at[0])]
    share = []
    for b in range(3):
        used = sum((cube[i] == b).astype(jnp.int32) for i in range(4))
        share.append(0.5 * jnp.minimum(used, 1).astype(F32))
    a_groups = []
    for h in (0, 1):
        held = [weight[pl.ds(part_start(q), PART), cols(h)]]
        arrive(g_groups[h], grec.at[h])
        for delta in range(1, GROUP):
            held.append(grec[h, delta - 1].astype(F32))
        for b in range(3):
            held = [held[d] + share[b] * (held[d ^ (1 << b)] - held[d]) for d in range(GROUP)]
        a_groups.append(new_group())
        for delta in range(1, GROUP):
            gsend[h, delta - 1] = held[delta].astype(BF16)
            remote(gsend.at[h, delta - 1], arec.at[h, delta - 1], gossip_dev(delta), a_groups[h])
        averaged[h, pl.ds(part_start(q), PART), :] = held[0]
    for which in range(STEPS):
        flush(which)
    for h in (0, 1):
        arrive(a_groups[h], arec.at[h])
        for delta in range(1, GROUP):
            averaged[h, pl.ds(part_start(member(delta)), PART), :] = arec[h, delta - 1].astype(F32)
        outs.append(local(averaged.at[h], avg_out.at[0, :, cols(h)]))

    flush(STEPS)
    for copy in outs:
        loaded(copy)


def store_kernel(*refs):
    ins, outs, held, sems = refs[:3], refs[3:6], refs[6:9], refs[9]
    reads = [pltpu.make_async_copy(ins[i], held[i], sems.at[i]) for i in range(3)]
    writes = [pltpu.make_async_copy(held[i], outs[i], sems.at[3 + i]) for i in range(3)]
    for copy in reads:
        copy.start()
    for i in range(3):
        reads[i].wait()
        writes[i].start()
    for copy in writes:
        copy.wait()


def body(tokens, master, moment, second, cube_bit):
    any_space = pl.BlockSpec(memory_space=pl.ANY)
    rows = jax.ShapeDtypeStruct((1, ROWS, 2 * RANK), F32)
    scratch = [
        pltpu.VMEM((ROWS, 2 * RANK), F32),
        pltpu.VMEM((ROWS, 2 * RANK), F32),
        pltpu.VMEM((ROWS, 2 * RANK), F32),
        pltpu.VMEM((STEPS + 1, 2, 2, CHIP_ROWS, RANK), BF16),
        pltpu.VMEM((STEPS, DOC, D), BF16),
        pltpu.VMEM((STEPS, 2, YS * DOC, CHIP_ROWS), BF16),
        pltpu.VMEM((2, CHIP_ROWS, YS * DOC), BF16),
        pltpu.VMEM((STEPS, DOC, DOC), F32),
        pltpu.VMEM((2, YS, DOC, RANK), F32),
        pltpu.VMEM((STEPS, RANK, RANK), BF16),
        pltpu.VMEM((STEPS, 3, RANK, RANK), BF16),
        pltpu.VMEM((STEPS, 2, 3, DOC, RANK), BF16),
        pltpu.VMEM((STEPS, 2, 3, DOC, RANK), BF16),
        pltpu.VMEM((STEPS, 3, YS, DOC, RANK), BF16),
        pltpu.VMEM((CHIP_ROWS, RANK), BF16),
        pltpu.VMEM((ROWS, RANK), F32),
        pltpu.VMEM((2, ROWS, RANK), F32),
        pltpu.VMEM((STEPS, 2, 2, ROWS, RANK), BF16),
        pltpu.VMEM((STEPS, 2, 2, ROWS, RANK), BF16),
        pltpu.VMEM((STEPS, 2, ROWS, RANK), BF16),
        pltpu.VMEM((STEPS, 2, ROWS, RANK), BF16),
        pltpu.VMEM((2, GROUP - 1, PART, RANK), BF16),
        pltpu.VMEM((2, GROUP - 1, PART, RANK), BF16),
        pltpu.VMEM((2, GROUP - 1, PART, RANK), BF16),
        pltpu.VMEM((2, ROWS, RANK), F32),
        pltpu.VMEM((BULK, RANK), BF16),
        pltpu.SemaphoreType.DMA((STEPS + 1,)),
        pltpu.SemaphoreType.DMA((N_GROUPS,)),
        pltpu.SemaphoreType.DMA((N_LOCAL,)),
        pltpu.SemaphoreType.REGULAR,
        pltpu.SemaphoreType.REGULAR,
    ]
    outs = pl.pallas_call(
        kernel,
        out_shape=(rows, rows, rows),
        in_specs=[any_space] * 4 + [pl.BlockSpec(memory_space=pltpu.SMEM)],
        out_specs=(any_space,) * 3,
        scratch_shapes=scratch,
        compiler_params=pltpu.CompilerParams(
            collective_id=0, has_side_effects=True, vmem_limit_bytes=VMEM_LIMIT
        ),
        name="train",
    )(tokens, master, moment, second, cube_bit)
    return pl.pallas_call(
        store_kernel,
        out_shape=(rows, rows, rows),
        in_specs=[any_space] * 3,
        out_specs=(any_space,) * 3,
        scratch_shapes=[pltpu.VMEM((1, ROWS, 2 * RANK), F32)] * 3 + [pltpu.SemaphoreType.DMA((6,))],
        compiler_params=pltpu.CompilerParams(vmem_limit_bytes=VMEM_LIMIT),
        name="store",
    )(*outs)


def solution(mesh):
    in_specs = (
        P(None, "gossip", "fsdp", None),
        P("gossip", "fsdp", None),
        P("gossip", "fsdp", None),
        P("gossip", "fsdp", None),
        P(),
    )
    out_specs = (P("gossip", "fsdp", None), P("gossip", "fsdp", None), P("gossip", "fsdp", None))
    return jax.shard_map(body, mesh=mesh, in_specs=in_specs, out_specs=out_specs, check_vma=False)
```

time: 457 us -> 90.2 us (0.20)
  waiting for transfers between devices: 367 us -> 0 us
  Pallas kernels: 0 us -> 88.8 us
  other arithmetic: 28.7 us -> 0 us
  local copies, waits for them, and re-layouts: 23 us -> 0 us
  matrix products: 18.2 us -> 0 us
  between operations: 16.5 us -> 0.64 us
    reduce_scatter x2 -> x0, waiting for transfers between devices: 212 us -> none  [body(): lax.psum_scatter(jnp.concatenate([jnp.einsum('td,tr->dr', normed, d_low,...]
    all_gather x2 -> x0, waiting for transfers between devices: 126 us -> none  [body(): lax.all_gather(params.astype(jnp.bfloat16), 'fsdp', axis=0, tiled=True)]
    pallas_call x0 -> x2, Pallas kernels: none -> 88.8 us  [the longest x1 86.8 us: body(): pl.pallas_call(kernel, out_shape=(rows, rows, rows), in_specs=[any_space]...]
    ppermute x4 -> x0, waiting for transfers between devices: 28.9 us -> none  [partner(): return lax.ppermute(value, axis, pairs)]
    dot_general x8 -> x0, matrix products: 18.2 us -> none  [the longest x2 8.6 us: body(): jnp.einsum('td,tr->dr', normed, d_low, preferred_element_type=jnp.float32)]
    unnamed x26 -> x0, local copies, waits for them, and re-layouts: 17 us -> none
    concatenate x2 -> x0, other arithmetic: 10.9 us -> none  [body(): jnp.concatenate([jnp.einsum('td,tr->dr', normed, d_low, preferred_element...]
    slice x3 -> x0, local copies, waits for them, and re-layouts: 5.92 us -> none  [the longest x2 5.3 us: body(): scaled[1:]]
  transfers between devices with their start and end apart: 8 -> 0, of which waited for: 8 -> 0; matrix products, arithmetic and copies ran while one was open for 2% -> 0% of each run, Pallas kernels for 0% -> 0%
where the time goes in v2:
time: 90.2 us; the launch traced here: 89.4 us
  Pallas kernels  88.8 us (98%)
    pallas_call x1, Pallas kernels, body(): pl.pallas_call(kernel, out_shape=(rows, rows, rows), in_specs=[any_space]...  86.8 us
    pallas_call x1, Pallas kernels, body(): pl.pallas_call(store_kernel, out_shape=(rows, rows, rows), in_specs=[any_...  1.96 us

profile of v2, /device:TPU:2, one launch (start us, length us, event | category | flops | bytes accessed | tf_op | source)
XLA Modules:
  0.0 89.4 jit_solution(7106469872958910528)
XLA Ops:
  0.6 86.8 %train.1 = (f32[1,320,256]{2,1,0:T(8,128)}, f32[1,320,256]{2,1,0:T(8,128)}, f32[1,320,256]{2,1,0:T(8,128)}) custom-call(bf16[2,1,128,5120]{3,2,1,0:T(8,128)(2,1)} %tokens.1, f32[1,320,256]{2,1,0:T(8,128)} %master.1, f32[1,320,256]{2,1,0:T(8,128)} %moment.1, f32[1,320,256]{2,1,0:T(8,128)} %second.1, s32[4]{0:T(128)} %cube.1), custom_call_target="tpu_custom_call" | custom-call | tf_op jit(solution)/shard_map/train/pallas_call | solution.py:470
  87.4 2.0 %store.1 = (f32[1,320,256]{2,1,0:T(8,128)}, f32[1,320,256]{2,1,0:T(8,128)}, f32[1,320,256]{2,1,0:T(8,128)}) custom-call(f32[1,320,256]{2,1,0:T(8,128)} %get-tuple-element.6.refs_0_, f32[1,320,256]{2,1,0:T(8,128)} %get-tuple-element.7.refs_1_, f32[1,320,256]{2,1,0:T(8,128)} %get-tuple-element.8.refs_2_), custom_call_target="tpu_custom_call" | custom-call | tf_op jit(solution)/shard_map/store/pallas_call | solution.py:481

commit v3 on v2

--- a/solution.py
+++ b/solution.py
@@ -21,7 +21,7 @@
 YS = 4
 GROUP = 8
 PART = 48
-N_GROUPS = 46
+N_GROUPS = 47
 N_LOCAL = 13
 BULK = 12288
 VMEM_LIMIT = 60 * 1024 * 1024
@@ -34,7 +34,7 @@
 
 def kernel(
     tokens, master, moment, second, cube, avg_out, mom_out, sec_out,
-    weight, first, squares, wire, docs, xs, xt, xgram, pacc, gram_send, gram_recv, psend, prec, eall, right,
+    weight, first, squares, wire, docs, xs, xt, xgram, pacc, wide, gram_send, gram_recv, half_send, half_recv, psend, prec, eall, right,
     keep_cross, keep_own, dsend, drec, zsend, zrec, grec, gsend, arec, averaged,
     bulk, send_sem, recv_sem, local_sem, near_sem, far_sem,
 ):
@@ -157,13 +157,9 @@
         return lax.dot_general(a, b, (((0,), (0,)), ((), ())), preferred_element_type=F32)
 
     def send_tokens(s):
-        groups = {}
-        for k in OTHERS:
-            groups[k] = new_group()
-            for p in (0, 1):
-                remote(
-                    docs.at[s, :, feature_cols(p, y_peer(k))], xs.at[s, p, doc_rows(y), :], y_dev(k), groups[k]
-                )
+        groups = {k: new_group() for k in OTHERS}
+        for k, p in ((1, 0), (3, 0), (1, 1), (3, 1), (2, 0), (2, 1)):
+            remote(docs.at[s, :, feature_cols(p, y_peer(k))], xs.at[s, p, doc_rows(y), :], y_dev(k), groups[k])
         return groups
 
     def send_weights(s, h):
@@ -217,8 +213,8 @@
         def part_product(who, h, p):
             return dot(xs[s, p, doc_rows(who), :], wire[s, h, p])
 
-        def part_gram(p):
-            right[...] = wire[s, 1, p]
+        def part_gram(p, core):
+            right[...] = wire[s, 1, p, rows_of(core), :]
             return tdot(right[...], right[...])
 
         def tokens_here(k):
@@ -230,6 +226,12 @@
             gram_send[s] = gram.astype(BF16)
             for k in OTHERS:
                 remote(gram_send.at[s], gram_recv.at[s, k - 1], y_dev(k), gram_group)
+
+        def gram_sum(gram):
+            arrive(gram_group, gram_recv.at[s])
+            for k in range(3):
+                gram += gram_recv[s, k].astype(F32)
+            return gram
 
         def send_product(k, h, value):
             psend[s, h, k - 1] = value.astype(BF16)
@@ -240,35 +242,47 @@
             for h in (0, 1):
                 weights_here(w_groups[h][1], s, h, z)
                 weights_here(forwards[h], s, h, 1 - z)
-            gram = part_gram(0) + part_gram(1)
+            gram = sum(part_gram(p, core) for p in (0, 1) for core in (0, 1))
             send_gram(gram)
             for copy in in_own[s]:
                 loaded(copy)
+            for p in (0, 1):
+                wide[p] = jnp.concatenate([wire[s, 0, p], wire[s, 1, p]], axis=1)
+
+            def whole_product(who):
+                return sum(dot(xs[s, p, doc_rows(who), :], wide[p]) for p in (0, 1))
+
             for k in OTHERS:
                 tokens_here(YS - k)
+                value = whole_product(y_peer(k))
                 for h in (0, 1):
-                    send_product(k, h, part_product(y_peer(k), h, 0) + part_product(y_peer(k), h, 1))
+                    send_product(k, h, value[:, cols(h)])
+            value = whole_product(y)
             for h in (0, 1):
-                pacc[h, 0] = part_product(y, h, 0) + part_product(y, h, 1)
+                pacc[h, 0] = value[:, cols(h)]
         else:
             for copy in in_own[s]:
                 loaded(copy)
             for k in OTHERS:
                 tokens_here(k)
+            weights_here(w_groups[1][1], s, 1, z)
+            gram = part_gram(z, c) + part_gram(z, 1 - c)
+            send_gram(gram)
             weights_here(w_groups[0][1], s, 0, z)
             for k in range(YS):
                 pacc[0, k] = part_product(y_peer(k), 0, z)
-            weights_here(forward_weights(s, 0), s, 0, 1 - z)
+                pacc[1, k] = part_product(y_peer(k), 1, z)
+            forward = forward_weights(s, 0)
+            gram = gram_sum(gram)
+            half_send[...] = gram.astype(BF16)
+            half_group = new_group()
+            remote(half_send, half_recv, z_dev, half_group)
+            weights_here(forward, s, 0, 1 - z)
             for k in OTHERS:
                 send_product(k, 0, pacc[0, k] + part_product(y_peer(k), 0, 1 - z))
             pacc[0, 0] += part_product(y, 0, 1 - z)
-            weights_here(w_groups[1][1], s, 1, z)
-            for k in range(YS):
-                pacc[1, k] = part_product(y_peer(k), 1, z)
-            gram = part_gram(z)
-            weights_here(forward_weights(s, 1), s, 1, 1 - z)
-            gram += part_gram(1 - z)
-            send_gram(gram)
+            forward = forward_weights(s, 1)
+            weights_here(forward, s, 1, 1 - z)
             for k in OTHERS:
                 send_product(k, 1, pacc[1, k] + part_product(y_peer(k), 1, 1 - z))
             pacc[1, 0] += part_product(y, 1, 1 - z)
@@ -284,9 +298,11 @@
         ixn = pltpu.roll(jnp.broadcast_to(ix, tall), DOC - 1, 0)[:, :1]
         kept = jnp.where(lax.broadcasted_iota(jnp.int32, (DOC, 1), 0) == DOC - 1, 0.0, alpha)
 
-        arrive(gram_group, gram_recv.at[s])
-        for k in range(3):
-            gram += gram_recv[s, k].astype(F32)
+        if s == 0:
+            gram = gram_sum(gram)
+        else:
+            arrive(half_group, half_recv)
+            gram += half_recv[...].astype(F32)
         ghi = gram.astype(BF16)
         glo = (gram - ghi.astype(F32)).astype(BF16)
         arrive(p_groups[0], prec.at[s, 0])
@@ -329,7 +345,6 @@
             stage[0] = s + 1
             loaded(in_doc[s + 1])
             tok_groups.append(send_tokens(s + 1))
-
         own_groups = []
         z_groups = []
         for h in (0, 1):
@@ -444,12 +459,15 @@
         pltpu.VMEM((2, CHIP_ROWS, YS * DOC), BF16),
         pltpu.VMEM((STEPS, DOC, DOC), F32),
         pltpu.VMEM((2, YS, DOC, RANK), F32),
+        pltpu.VMEM((2, CHIP_ROWS, 2 * RANK), BF16),
         pltpu.VMEM((STEPS, RANK, RANK), BF16),
         pltpu.VMEM((STEPS, 3, RANK, RANK), BF16),
+        pltpu.VMEM((RANK, RANK), BF16),
+        pltpu.VMEM((RANK, RANK), BF16),
         pltpu.VMEM((STEPS, 2, 3, DOC, RANK), BF16),
         pltpu.VMEM((STEPS, 2, 3, DOC, RANK), BF16),
         pltpu.VMEM((STEPS, 3, YS, DOC, RANK), BF16),
-        pltpu.VMEM((CHIP_ROWS, RANK), BF16),
+        pltpu.VMEM((ROWS, RANK), BF16),
         pltpu.VMEM((ROWS, RANK), F32),
         pltpu.VMEM((2, ROWS, RANK), F32),
         pltpu.VMEM((STEPS, 2, 2, ROWS, RANK), BF16),

time: 90.2 us -> 89 us (0.987)
  no operation moved by 1% of the time
where the time goes in v3:
time: 89 us; the launch traced here: 88.5 us
  Pallas kernels  87.9 us (99%)
    pallas_call x1, Pallas kernels, body(): pl.pallas_call(kernel, out_shape=(rows, rows, rows), in_specs=[any_space]...  85.9 us
    pallas_call x1, Pallas kernels, body(): pl.pallas_call(store_kernel, out_shape=(rows, rows, rows), in_specs=[any_...  1.96 us

profile of v3, /device:TPU:2, one launch (start us, length us, event | category | flops | bytes accessed | tf_op | source)
XLA Modules:
  0.0 88.5 jit_solution(15808726327305200666)
XLA Ops:
  0.6 85.9 %train.1 = (f32[1,320,256]{2,1,0:T(8,128)}, f32[1,320,256]{2,1,0:T(8,128)}, f32[1,320,256]{2,1,0:T(8,128)}) custom-call(bf16[2,1,128,5120]{3,2,1,0:T(8,128)(2,1)} %tokens.1, f32[1,320,256]{2,1,0:T(8,128)} %master.1, f32[1,320,256]{2,1,0:T(8,128)} %moment.1, f32[1,320,256]{2,1,0:T(8,128)} %second.1, s32[4]{0:T(128)} %cube.1), custom_call_target="tpu_custom_call" | custom-call | tf_op jit(solution)/shard_map/train/pallas_call | solution.py:488
  86.5 2.0 %store.1 = (f32[1,320,256]{2,1,0:T(8,128)}, f32[1,320,256]{2,1,0:T(8,128)}, f32[1,320,256]{2,1,0:T(8,128)}) custom-call(f32[1,320,256]{2,1,0:T(8,128)} %get-tuple-element.6.refs_0_, f32[1,320,256]{2,1,0:T(8,128)} %get-tuple-element.7.refs_1_, f32[1,320,256]{2,1,0:T(8,128)} %get-tuple-element.8.refs_2_), custom_call_target="tpu_custom_call" | custom-call | tf_op jit(solution)/shard_map/store/pallas_call | solution.py:499

commit v4 on v3

--- a/solution.py
+++ b/solution.py
@@ -21,7 +21,7 @@
 YS = 4
 GROUP = 8
 PART = 48
-N_GROUPS = 47
+N_GROUPS = 27
 N_LOCAL = 13
 BULK = 12288
 VMEM_LIMIT = 60 * 1024 * 1024
@@ -34,7 +34,8 @@
 
 def kernel(
     tokens, master, moment, second, cube, avg_out, mom_out, sec_out,
-    weight, first, squares, wire, docs, xs, xt, xgram, pacc, wide, gram_send, gram_recv, half_send, half_recv, psend, prec, eall, right,
+    weight, first, squares, wire, docs, xs, xt, xgram, pacc, wide, gram_send, gram_recv, half_send, half_recv,
+    gram_full, core_gram_send, core_gram_recv, psend, prec, eall, right,
     keep_cross, keep_own, dsend, drec, zsend, zrec, grec, gsend, arec, averaged,
     bulk, send_sem, recv_sem, local_sem, near_sem, far_sem,
 ):
@@ -102,8 +103,13 @@
     stage = [0]
     bytes_sent = [0] * (STEPS + 1)
 
-    def new_group():
+    named = {}
+
+    def new_group(*name):
+        if name and name in named:
+            return named[name]
         count[0] += 1
+        named[name] = count[0] - 1
         return count[0] - 1
 
     def remote(src, dst, device, group):
@@ -150,6 +156,9 @@
     def cols(h):
         return slice(h * RANK, (h + 1) * RANK)
 
+    my_half = pl.ds(pl.multiple_of(c * (RANK // 2), RANK // 2), RANK // 2)
+    other_half = pl.ds(pl.multiple_of((1 - c) * (RANK // 2), RANK // 2), RANK // 2)
+
     def dot(a, b):
         return jnp.dot(a, b, preferred_element_type=F32)
 
@@ -157,21 +166,21 @@
         return lax.dot_general(a, b, (((0,), (0,)), ((), ())), preferred_element_type=F32)
 
     def send_tokens(s):
-        groups = {k: new_group() for k in OTHERS}
+        groups = {k: new_group("tok", k) for k in OTHERS}
         for k, p in ((1, 0), (3, 0), (1, 1), (3, 1), (2, 0), (2, 1)):
             remote(docs.at[s, :, feature_cols(p, y_peer(k))], xs.at[s, p, doc_rows(y), :], y_dev(k), groups[k])
         return groups
 
     def send_weights(s, h):
         own = wire.at[s, h, z, rows_of(c), :]
-        groups = new_group(), new_group()
+        groups = new_group("wz", h), new_group("wc", h)
         remote(own, own, z_dev, groups[0])
         remote(own, own, core_dev, groups[1])
         return groups
 
     def forward_weights(s, h):
         got = wire.at[s, h, 1 - z, rows_of(c), :]
-        group = new_group()
+        group = new_group("wf", h)
         arrive(w_groups[h][0], got)
         remote(got, got, core_dev, group)
         return group
@@ -220,7 +229,7 @@
         def tokens_here(k):
             arrive(tok_groups[s][k], xs.at[s, :, doc_rows((y + YS - k) % YS), :])
 
-        gram_group, p_groups = new_group(), (new_group(), new_group())
+        gram_group, p_groups = new_group("gram"), (new_group("p", 0), new_group("p", 1))
 
         def send_gram(gram):
             gram_send[s] = gram.astype(BF16)
@@ -242,8 +251,10 @@
             for h in (0, 1):
                 weights_here(w_groups[h][1], s, h, z)
                 weights_here(forwards[h], s, h, 1 - z)
-            gram = sum(part_gram(p, core) for p in (0, 1) for core in (0, 1))
-            send_gram(gram)
+            gram_full[...] = sum(part_gram(p, core) for p in (0, 1) for core in (0, 1))
+            core_gram_send[0] = gram_full[my_half, :].astype(BF16)
+            for k in OTHERS:
+                remote(core_gram_send.at[0], core_gram_recv.at[k - 1], y_dev(k), gram_group)
             for copy in in_own[s]:
                 loaded(copy)
             for p in (0, 1):
@@ -257,18 +268,24 @@
                 value = whole_product(y_peer(k))
                 for h in (0, 1):
                     send_product(k, h, value[:, cols(h)])
+            arrive(gram_group, core_gram_recv.at[pl.ds(0, 3)])
+            half_sum = gram_full[my_half, :] + sum(core_gram_recv[k].astype(F32) for k in range(3))
+            core_gram_send[1] = half_sum.astype(BF16)
+            half_group = new_group()
+            remote(core_gram_send.at[1], core_gram_recv.at[3], core_dev, half_group)
+            gram_full[my_half, :] = half_sum
             value = whole_product(y)
             for h in (0, 1):
                 pacc[h, 0] = value[:, cols(h)]
         else:
-            for copy in in_own[s]:
-                loaded(copy)
-            for k in OTHERS:
-                tokens_here(k)
             weights_here(w_groups[1][1], s, 1, z)
             gram = part_gram(z, c) + part_gram(z, 1 - c)
             send_gram(gram)
             weights_here(w_groups[0][1], s, 0, z)
+            for copy in in_own[s]:
+                loaded(copy)
+            for k in OTHERS:
+                tokens_here(k)
             for k in range(YS):
                 pacc[0, k] = part_product(y_peer(k), 0, z)
                 pacc[1, k] = part_product(y_peer(k), 1, z)
@@ -299,7 +316,9 @@
         kept = jnp.where(lax.broadcasted_iota(jnp.int32, (DOC, 1), 0) == DOC - 1, 0.0, alpha)
 
         if s == 0:
-            gram = gram_sum(gram)
+            arrive(half_group, core_gram_recv.at[3])
+            gram_full[other_half, :] = core_gram_recv[3].astype(F32)
+            gram = gram_full[...]
         else:
             arrive(half_group, half_recv)
             gram += half_recv[...].astype(F32)
@@ -333,7 +352,7 @@
 
         def send_factor(kind, value):
             eall[s, kind, y] = value.astype(BF16)
-            e_groups.append(new_group())
+            e_groups.append(new_group("e", kind))
             for k in OTHERS:
                 remote(eall.at[s, kind, y], eall.at[s, kind, y], y_dev(k), e_groups[kind])
 
@@ -361,15 +380,15 @@
                 return rows
 
             dsend[s, h, 0] = gradient(1 - z, 1 - c).astype(BF16)
-            cross = new_group()
+            cross = new_group("cross", h)
             remote(dsend.at[s, h, 0], drec.at[s, h, 0], core_dev, cross)
             keep_cross[...] = gradient(1 - z, c)
             dsend[s, h, 1] = gradient(z, 1 - c).astype(BF16)
-            own_groups.append(new_group())
+            own_groups.append(new_group("own", h))
             remote(dsend.at[s, h, 1], drec.at[s, h, 1], core_dev, own_groups[h])
             arrive(cross, drec.at[s, h, 0])
             zsend[s, h] = (keep_cross[...] + drec[s, h, 0].astype(F32)).astype(BF16)
-            z_groups.append(new_group())
+            z_groups.append(new_group("z", h))
             remote(zsend.at[s, h], zrec.at[s, h], z_dev, z_groups[h])
             keep_own[h] = gradient(z, c)
         if s == 0:
@@ -464,6 +483,9 @@
         pltpu.VMEM((STEPS, 3, RANK, RANK), BF16),
         pltpu.VMEM((RANK, RANK), BF16),
         pltpu.VMEM((RANK, RANK), BF16),
+        pltpu.VMEM((RANK, RANK), F32),
+        pltpu.VMEM((2, RANK // 2, RANK), BF16),
+        pltpu.VMEM((4, RANK // 2, RANK), BF16),
         pltpu.VMEM((STEPS, 2, 3, DOC, RANK), BF16),
         pltpu.VMEM((STEPS, 2, 3, DOC, RANK), BF16),
         pltpu.VMEM((STEPS, 3, YS, DOC, RANK), BF16),

time: 89 us -> 88.5 us (level)
  no operation moved by 1% of the time
where the time goes in v4:
time: 88.5 us; the launch traced here: 88.1 us
  Pallas kernels  87.5 us (99%)
    pallas_call x1, Pallas kernels, body(): pl.pallas_call(kernel, out_shape=(rows, rows, rows), in_specs=[any_space]...  85.5 us
    pallas_call x1, Pallas kernels, body(): pl.pallas_call(store_kernel, out_shape=(rows, rows, rows), in_specs=[any_...  1.96 us

profile of v4, /device:TPU:2, one launch (start us, length us, event | category | flops | bytes accessed | tf_op | source)
XLA Modules:
  0.0 88.1 jit_solution(7277906285611894663)
XLA Ops:
  0.6 85.5 %train.1 = (f32[1,320,256]{2,1,0:T(8,128)}, f32[1,320,256]{2,1,0:T(8,128)}, f32[1,320,256]{2,1,0:T(8,128)}) custom-call(bf16[2,1,128,5120]{3,2,1,0:T(8,128)(2,1)} %tokens.1, f32[1,320,256]{2,1,0:T(8,128)} %master.1, f32[1,320,256]{2,1,0:T(8,128)} %moment.1, f32[1,320,256]{2,1,0:T(8,128)} %second.1, s32[4]{0:T(128)} %cube.1), custom_call_target="tpu_custom_call" | custom-call | tf_op jit(solution)/shard_map/train/pallas_call | solution.py:510
  86.2 2.0 %store.1 = (f32[1,320,256]{2,1,0:T(8,128)}, f32[1,320,256]{2,1,0:T(8,128)}, f32[1,320,256]{2,1,0:T(8,128)}) custom-call(f32[1,320,256]{2,1,0:T(8,128)} %get-tuple-element.6.refs_0_, f32[1,320,256]{2,1,0:T(8,128)} %get-tuple-element.7.refs_1_, f32[1,320,256]{2,1,0:T(8,128)} %get-tuple-element.8.refs_2_), custom_call_target="tpu_custom_call" | custom-call | tf_op jit(solution)/shard_map/store/pallas_call | solution.py:521

commit v5 on v4

--- a/solution.py
+++ b/solution.py
@@ -305,7 +305,8 @@
             pacc[1, 0] += part_product(y, 1, 1 - z)
 
         for p in (0, 1):
-            xt[p] = xs[s, p].T
+            xt[p, :, : YS * DOC] = xs[s, p].T
+            xt[p, :, YS * DOC :] = wire[s, 1, p]
         at_t = lax.broadcasted_iota(jnp.int32, tall, 0)
         at_j = lax.broadcasted_iota(jnp.int32, tall, 1)
         xx = xgram[s]
@@ -372,12 +373,10 @@
             factor = eall[s, h].reshape(YS * DOC, RANK)
             if h == 1:
                 outer = sum(eall[s, 2, j].astype(F32) for j in range(YS)).astype(BF16)
+                factor = jnp.concatenate([factor, outer], axis=0)
 
             def gradient(p, core):
-                rows = dot(xt[p, rows_of(core), :], factor)
-                if h == 1:
-                    rows += dot(wire[s, 1, p, rows_of(core), :], outer)
-                return rows
+                return dot(xt[p, rows_of(core), : factor.shape[0]], factor)
 
             dsend[s, h, 0] = gradient(1 - z, 1 - c).astype(BF16)
             cross = new_group("cross", h)
@@ -475,7 +474,7 @@
         pltpu.VMEM((STEPS + 1, 2, 2, CHIP_ROWS, RANK), BF16),
         pltpu.VMEM((STEPS, DOC, D), BF16),
         pltpu.VMEM((STEPS, 2, YS * DOC, CHIP_ROWS), BF16),
-        pltpu.VMEM((2, CHIP_ROWS, YS * DOC), BF16),
+        pltpu.VMEM((2, CHIP_ROWS, YS * DOC + RANK), BF16),
         pltpu.VMEM((STEPS, DOC, DOC), F32),
         pltpu.VMEM((2, YS, DOC, RANK), F32),
         pltpu.VMEM((2, CHIP_ROWS, 2 * RANK), BF16),

time: 88.5 us -> 88.6 us (level)
  no operation moved by 1% of the time
where the time goes in v5:
time: 88.6 us; the launch traced here: 88.2 us
  Pallas kernels  87.5 us (99%)
    pallas_call x1, Pallas kernels, body(): pl.pallas_call(kernel, out_shape=(rows, rows, rows), in_specs=[any_space]...  85.6 us
    pallas_call x1, Pallas kernels, body(): pl.pallas_call(store_kernel, out_shape=(rows, rows, rows), in_specs=[any_...  1.96 us

profile of v5, /device:TPU:2, one launch (start us, length us, event | category | flops | bytes accessed | tf_op | source)
XLA Modules:
  0.0 88.2 jit_solution(17411803888726520429)
XLA Ops:
  0.6 85.6 %train.1 = (f32[1,320,256]{2,1,0:T(8,128)}, f32[1,320,256]{2,1,0:T(8,128)}, f32[1,320,256]{2,1,0:T(8,128)}) custom-call(bf16[2,1,128,5120]{3,2,1,0:T(8,128)(2,1)} %tokens.1, f32[1,320,256]{2,1,0:T(8,128)} %master.1, f32[1,320,256]{2,1,0:T(8,128)} %moment.1, f32[1,320,256]{2,1,0:T(8,128)} %second.1, s32[4]{0:T(128)} %cube.1), custom_call_target="tpu_custom_call" | custom-call | tf_op jit(solution)/shard_map/train/pallas_call | solution.py:509
  86.2 2.0 %store.1 = (f32[1,320,256]{2,1,0:T(8,128)}, f32[1,320,256]{2,1,0:T(8,128)}, f32[1,320,256]{2,1,0:T(8,128)}) custom-call(f32[1,320,256]{2,1,0:T(8,128)} %get-tuple-element.6.refs_0_, f32[1,320,256]{2,1,0:T(8,128)} %get-tuple-element.7.refs_1_, f32[1,320,256]{2,1,0:T(8,128)} %get-tuple-element.8.refs_2_), custom_call_target="tpu_custom_call" | custom-call | tf_op jit(solution)/shard_map/store/pallas_call | solution.py:520
